TPU v7x, 32 devices: a whole 2x2x4 slice. The times are simulated.
32 devices in a mesh: parts: 2 (over x), seq: 16 (over z, y, core).
Axes of the slice: x: 2, y: 2, z: 4, core: 2. Of those that a mesh axis runs over, the one named last changes fastest.
Arguments:
- queries: bfloat16 [4096, 8192], P(('parts', 'seq')), parts along dimension 0, may hold values from -128 to 128
- keys: bfloat16 [4096, 1024], P(('parts', 'seq')), parts along dimension 0, may hold values from -6 to 6
- values: bfloat16 [4096, 1024], P(('parts', 'seq')), parts along dimension 0, may hold values from -6 to 6
- stream_block: int32 [256], P(('parts', 'seq')), parts along dimension 0, may hold values from 0 to 127, as said below
- segment_ids: int32 [4096], P('parts'), parts along dimension 0, may hold values from 0 to 3, never falling along the last dimension, each value on 1 to 1536 neighbouring positions
Outputs:
- attended: bfloat16 [4096, 8192], P(('parts', 'seq')), parts along dimension 0
There are 2 independent parts, one for each index of `parts`. A program takes and returns all parts, laid end to end along the dimension named above; each array names one. Nothing has to cross between parts.
Inputs may be any that keep to these rules, and one draw needn't show every extreme that they name: `stream_block`: A permutation of the numbers of the 128 blocks. Block number b lies in the share of device floor(b / 8) of the joined sequences. The blocks loaded by one device land in the shares of 8 different devices, at most one block in each, and every device's share takes one block from each of 8 loading devices.
All inputs are finite; a program needn't handle non-finite values.
Results may differ from a plain program's by a relative error of at most 0.004.
Values may be sent and summed in bfloat16 or wider, within the bound.
A program may use at most 64 MiB of HBM per device.

v0:
```python
import jax
import jax.numpy as jnp
from jax import lax
from jax.sharding import PartitionSpec as P

KVH = 8
HD = 128


masked_floor = -1e30
tile_rows = 512


def segment_starts(segment_ids):
    places = jnp.arange(segment_ids.shape[0], dtype=jnp.int32)
    fresh = jnp.concatenate([jnp.ones((1,), jnp.bool_), segment_ids[1:] != segment_ids[:-1]])
    return lax.cummax(jnp.where(fresh, places, 0), axis=0)


def blocks_for_peers(rows, owners, peer_count):
    count = owners.shape[0]
    shaped = rows.reshape(count, rows.shape[0] // count, rows.shape[1])
    match = owners[None, :] == jnp.arange(peer_count, dtype=jnp.int32)[:, None]
    choose = jnp.sum(jnp.where(match, jnp.arange(count, dtype=jnp.int32)[None, :], 0), axis=1)
    present = jnp.any(match, axis=1)
    return jnp.where(present[:, None, None], shaped[choose], jnp.zeros((), rows.dtype))


def attend(head_queries, head_keys, head_values, segment_ids):
    total, width = head_queries.shape
    per_device = width // HD
    scale = HD ** (-0.5)
    starts = segment_starts(segment_ids)
    places = jnp.arange(total, dtype=jnp.int32)

    def query_tile(tile_index):
        first = tile_index * tile_rows
        query_block = lax.dynamic_slice_in_dim(head_queries, first, tile_rows, 0).reshape(
            tile_rows * per_device, HD
        )
        query_places = jnp.repeat(lax.dynamic_slice_in_dim(places, first, tile_rows, 0), per_device)
        query_segments = jnp.repeat(
            lax.dynamic_slice_in_dim(segment_ids, first, tile_rows, 0), per_device
        )
        lowest = lax.dynamic_index_in_dim(starts, first, 0, keepdims=False) // tile_rows

        def key_step(key_tile, state):
            running, totals, sums = state
            key_first = key_tile * tile_rows
            key_block = lax.dynamic_slice_in_dim(head_keys, key_first, tile_rows, 0)
            value_block = lax.dynamic_slice_in_dim(head_values, key_first, tile_rows, 0)
            key_places = lax.dynamic_slice_in_dim(places, key_first, tile_rows, 0)
            key_segments = lax.dynamic_slice_in_dim(segment_ids, key_first, tile_rows, 0)
            scores = (
                jnp.einsum("qd,kd->qk", query_block, key_block, preferred_element_type=jnp.float32)
                * scale
            )
            allowed = (query_segments[:, None] == key_segments[None, :]) & (
                key_places[None, :] <= query_places[:, None]
            )
            masked = jnp.where(allowed, scores, masked_floor)
            newest = jnp.maximum(running, jnp.max(masked, axis=1))
            weights = jnp.where(allowed, jnp.exp(masked - newest[:, None]), 0.0).astype(
                jnp.bfloat16
            )
            factor = jnp.exp(running - newest)
            totals = totals * factor + jnp.sum(weights.astype(jnp.float32), axis=1)
            sums = sums * factor[:, None] + jnp.dot(
                weights, value_block, preferred_element_type=jnp.float32
            )
            return (newest, totals, sums)

        rows_here = tile_rows * per_device
        initial = (
            jnp.full((rows_here,), masked_floor, jnp.float32),
            jnp.zeros((rows_here,), jnp.float32),
            jnp.zeros((rows_here, HD), jnp.float32),
        )
        running, totals, sums = lax.fori_loop(lowest, tile_index + 1, key_step, initial)
        return (sums / totals[:, None]).astype(jnp.bfloat16).reshape(tile_rows, width)

    outputs = lax.map(query_tile, jnp.arange(total // tile_rows, dtype=jnp.int32))
    return outputs.reshape(total, width)


def body(queries, keys, values, stream_block, segment_ids):
    devices = lax.axis_size("seq")
    self_index = lax.axis_index("seq")
    local_rows = queries.shape[0]
    own_blocks = stream_block.shape[0]
    all_blocks = lax.all_gather(stream_block, "seq", axis=0, tiled=True)
    total_blocks = all_blocks.shape[0]
    order = (
        jnp.zeros((total_blocks,), jnp.int32)
        .at[all_blocks]
        .set(jnp.arange(total_blocks, dtype=jnp.int32))
    )
    paired = jnp.concatenate([keys, values], axis=1)
    targets = stream_block // own_blocks
    outgoing = (
        blocks_for_peers(queries, targets, devices),
        blocks_for_peers(paired, targets, devices),
    )
    arrived_queries, arrived_pairs = (
        lax.all_to_all(outgoing[0], "seq", split_axis=0, concat_axis=0, tiled=True),
        lax.all_to_all(outgoing[1], "seq", split_axis=0, concat_axis=0, tiled=True),
    )
    slot_blocks = lax.dynamic_slice_in_dim(order, self_index * own_blocks, own_blocks, 0)
    sources = slot_blocks // own_blocks
    ready_queries = arrived_queries[sources].reshape(local_rows, queries.shape[1])
    ready_pairs = arrived_pairs[sources].reshape(local_rows, paired.shape[1])
    group = devices // KVH
    key_heads = ready_pairs[:, : KVH * HD].reshape(local_rows, KVH, HD)
    value_heads = ready_pairs[:, KVH * HD :].reshape(local_rows, KVH, HD)
    pair_heads = jnp.stack([key_heads, value_heads], axis=2)
    spread = jnp.repeat(pair_heads, group, axis=1).reshape(local_rows, devices * 2 * HD)
    head_queries, head_pairs = (
        lax.all_to_all(ready_queries, "seq", split_axis=1, concat_axis=0, tiled=True),
        lax.all_to_all(spread, "seq", split_axis=1, concat_axis=0, tiled=True),
    )
    attended = attend(head_queries, head_pairs[:, :HD], head_pairs[:, HD:], segment_ids)
    returned = lax.all_to_all(attended, "seq", split_axis=0, concat_axis=1, tiled=True)
    going_back = blocks_for_peers(returned, sources, devices)
    came_back = lax.all_to_all(going_back, "seq", split_axis=0, concat_axis=0, tiled=True)
    returned = came_back[targets].reshape(local_rows, returned.shape[1])
    return returned


def solution(mesh):
    placed = (
        P(("parts", "seq"), None),
        P(("parts", "seq"), None),
        P(("parts", "seq"), None),
        P(("parts", "seq")),
        P("parts"),
    )
    return jax.shard_map(
        body, mesh=mesh, in_specs=placed, out_specs=P(("parts", "seq"), None), check_vma=False
    )
```

profile of v0, /device:TPU:13, one launch (start us, length us, event | category | flops | bytes accessed | tf_op | source)
XLA Modules:
  0.0 484.7 jit_solution(7986711587501427439)
XLA Ops:
  4.1 2.3 broadcast_select_fusion.2
  6.5 6.6 %all-to-all-start.2 = ((bf16[16,16,2048]{2,1,0:T(8,128)(2,1)}), bf16[16,16,2048]{2,1,0:T(8,128)(2,1)S(1)}, u32[]{:S(2)}, u32[]{:S(2)}) async-start(bf16[16,16,2048]{2,1,0:T(8,128)(2,1)} %broadcast_select_fusion.2), calls=%async_computation.2 | async-start | bytes 2097152 | tf_op jit(solution)/shard_map/all_to_all | solution.py:106
  13.0 2.8 gather_fusion
  15.8 4.5 broadcast_select_fusion
  20.3 17.6 %all-to-all-done.2 = bf16[16,16,2048]{2,1,0:T(8,128)(2,1)S(1)} async-done(((bf16[16,16,2048]{2,1,0:T(8,128)(2,1)}), bf16[16,16,2048]{2,1,0:T(8,128)(2,1)S(1)}, u32[]{:S(2)}, u32[]{:S(2)}) %all-to-all-start.2) | async-done | bytes 1048608 | tf_op jit(solution)/shard_map/all_to_all | solution.py:106
  37.9 4.9 %all-to-all-start = ((bf16[16,16,8192]{2,1,0:T(8,128)(2,1)}), bf16[16,16,8192]{2,1,0:T(8,128)(2,1)}, u32[]{:S(2)}, u32[]{:S(2)}) async-start(bf16[16,16,8192]{2,1,0:T(8,128)(2,1)} %broadcast_select_fusion), calls=%async_computation | async-start | bytes 8388608 | tf_op jit(solution)/shard_map/all_to_all | solution.py:105
  44.3 88.9 %all-reduce = s32[128]{0:T(128)S(1)} all-reduce(s32[128]{0:T(128)S(1)} %dynamic-update-slice), channel_id=1, replica_groups=mesh['parts'=2,'seq'=16] {'seq'}, use_global_device_ids=true, to_apply=%add | all-reduce | flops 128 | bytes 1024
  139.9 7.5 %all-to-all-start.3 = ((bf16[128,16,256]{2,0,1:T(8,128)(2,1)}), bf16[128,16,256]{2,0,1:T(8,128)(2,1)S(1)}, u32[]{:S(2)}, u32[]{:S(2)}) async-start(bf16[128,16,256]{2,0,1:T(8,128)(2,1)} %all_to_all.55), calls=%async_computation.3 | async-start | bytes 2097152 | tf_op jit(solution)/shard_map/all_to_all | solution.py:119
  147.4 2.9 gather_fusion.1
  151.1 2.5 copy.19
  153.6 18.7 %all-to-all-done.3 = bf16[128,16,256]{2,0,1:T(8,128)(2,1)S(1)} async-done(((bf16[128,16,256]{2,0,1:T(8,128)(2,1)}), bf16[128,16,256]{2,0,1:T(8,128)(2,1)S(1)}, u32[]{:S(2)}, u32[]{:S(2)}) %all-to-all-start.3) | async-done | bytes 1048608 | tf_op jit(solution)/shard_map/all_to_all | solution.py:119
  172.3 4.9 %all-to-all-start.1 = ((bf16[128,16,512]{2,0,1:T(8,128)(2,1)}), bf16[128,16,512]{2,0,1:T(8,128)(2,1)}, u32[]{:S(2)}, u32[]{:S(2)}) async-start(bf16[128,16,512]{2,0,1:T(8,128)(2,1)} %copy.19), calls=%async_computation.1 | async-start | bytes 4194304 | tf_op jit(solution)/shard_map/all_to_all | solution.py:118
  178.9 45.9 %all-to-all-done.1 = bf16[128,16,512]{2,0,1:T(8,128)(2,1)} async-done(((bf16[128,16,512]{2,0,1:T(8,128)(2,1)}), bf16[128,16,512]{2,0,1:T(8,128)(2,1)}, u32[]{:S(2)}, u32[]{:S(2)}) %all-to-all-start.1) | async-done | bytes 2097184 | tf_op jit(solution)/shard_map/all_to_all | solution.py:118
  224.8 93.2 %while.42 = (s32[]{:T(128)}, bf16[4,512,512]{2,1,0:T(8,128)(2,1)}, s32[4]{0:T(128)S(1)}, s32[2048]{0:T(1024)S(1)}, bf16[2048,512]{1,0:T(8,128)(2,1)}, /*index=5*...) while((s32[]{:T(128)}, bf16[4,512,512]{2,1,0:T(8,128)(2,1)}, ...), condition=%wide.region_11.12_spmd.clone, body=%wide.region_6.11_spmd.clone.sunk | while | flops 554700800 | bytes 22541608 | solution.py:82
  231.3 6.1 %while.43 = (s32[]{:T(128)}, f32[2048]{0:T(1024)S(1)}, f32[2048]{0:T(1024)S(1)}, f32[2048,128]{1,0:T(8,128)S(1)}, s32[]{:T(128)}, /*index=5*/s32[2048]{0:T(1024)...) while((s32[]{:T(128)}, f32[2048]{0:T(1024)S(1)}, ...), condition=%wide.region_10.10_spmd.clone, body=%wide.region_7.9_spmd.clone.sunk | while | flops 554176512 | bytes 15691987 | solution.py:79
  234.2 2.1 convert_reduce_fusion.2
  245.5 12.2 %while.43 = (s32[]{:T(128)}, f32[2048]{0:T(1024)S(1)}, f32[2048]{0:T(1024)S(1)}, f32[2048,128]{1,0:T(8,128)S(1)}, s32[]{:T(128)}, /*index=5*/s32[2048]{0:T(1024)...) while((s32[]{:T(128)}, f32[2048]{0:T(1024)S(1)}, ...), condition=%wide.region_10.10_spmd.clone, body=%wide.region_7.9_spmd.clone.sunk | while | flops 554176512 | bytes 15691987 | solution.py:79
  248.3 2.1 convert_reduce_fusion.2
  254.4 2.1 convert_reduce_fusion.2
  265.7 18.2 %while.43 = (s32[]{:T(128)}, f32[2048]{0:T(1024)S(1)}, f32[2048]{0:T(1024)S(1)}, f32[2048,128]{1,0:T(8,128)S(1)}, s32[]{:T(128)}, /*index=5*/s32[2048]{0:T(1024)...) while((s32[]{:T(128)}, f32[2048]{0:T(1024)S(1)}, ...), condition=%wide.region_10.10_spmd.clone, body=%wide.region_7.9_spmd.clone.sunk | while | flops 554176512 | bytes 15691987 | solution.py:79
  268.6 2.1 convert_reduce_fusion.2
  274.7 2.1 convert_reduce_fusion.2
  292.0 24.3 %while.43 = (s32[]{:T(128)}, f32[2048]{0:T(1024)S(1)}, f32[2048]{0:T(1024)S(1)}, f32[2048,128]{1,0:T(8,128)S(1)}, s32[]{:T(128)}, /*index=5*/s32[2048]{0:T(1024)...) while((s32[]{:T(128)}, f32[2048]{0:T(1024)S(1)}, ...), condition=%wide.region_10.10_spmd.clone, body=%wide.region_7.9_spmd.clone.sunk | while | flops 554176512 | bytes 15691987 | solution.py:79
  317.9 5.0 %all-to-all-start.4 = ((bf16[16,128,512]{2,1,0:T(8,128)(2,1)}), bf16[16,128,512]{2,1,0:T(8,128)(2,1)S(1)}, u32[]{:S(2)}, u32[]{:S(2)}) async-start(bf16[16,128,512]{2,1,0:T(8,128)(2,1)} %bitcast.72), calls=%async_computation.4 | async-start | bytes 4194304 | tf_op jit(solution)/shard_map/all_to_all | solution.py:122
  323.1 47.2 %all-to-all-done.4 = bf16[16,128,512]{2,1,0:T(8,128)(2,1)S(1)} async-done(((bf16[16,128,512]{2,1,0:T(8,128)(2,1)}), bf16[16,128,512]{2,1,0:T(8,128)(2,1)S(1)}, u32[]{:S(2)}, u32[]{:S(2)}) %all-to-all-start.4) | async-done | bytes 2097184 | tf_op jit(solution)/shard_map/all_to_all | solution.py:122
  370.4 2.5 copy.22
  372.8 2.9 reshape.100
  375.7 2.8 gather_fusion.4
  378.5 4.5 broadcast_select_fusion.1
  383.0 5.0 %all-to-all-start.5 = ((bf16[16,16,8192]{2,1,0:T(8,128)(2,1)}), bf16[16,16,8192]{2,1,0:T(8,128)(2,1)}, u32[]{:S(2)}, u32[]{:S(2)}) async-start(bf16[16,16,8192]{2,1,0:T(8,128)(2,1)} %broadcast_select_fusion.1), calls=%async_computation.5 | async-start | bytes 8388608 | tf_op jit(solution)/shard_map/all_to_all | solution.py:124
  388.1 92.4 %all-to-all-done.5 = bf16[16,16,8192]{2,1,0:T(8,128)(2,1)} async-done(((bf16[16,16,8192]{2,1,0:T(8,128)(2,1)}), bf16[16,16,8192]{2,1,0:T(8,128)(2,1)}, u32[]{:S(2)}, u32[]{:S(2)}) %all-to-all-start.5) | async-done | bytes 4194336 | tf_op jit(solution)/shard_map/all_to_all | solution.py:124
  480.5 4.2 gather_fusion.5
  (219 shorter events, 81.0 us)
Async XLA Ops:
  0.0 13.0 %copy-start = (bf16[128,8192]{1,0:T(8,128)(2,1)S(1)}, bf16[128,8192]{1,0:T(8,128)(2,1)}, u32[]{:S(2)}) copy-start(bf16[128,8192]{1,0:T(8,128)(2,1)} %param.9) | copy-start | bytes 6291460
  6.5 31.4 %all-to-all-start.2 = ((bf16[16,16,2048]{2,1,0:T(8,128)(2,1)}), bf16[16,16,2048]{2,1,0:T(8,128)(2,1)S(1)}, u32[]{:S(2)}, u32[]{:S(2)}) async-start(bf16[16,16,2048]{2,1,0:T(8,128)(2,1)} %broadcast_select_fusion.2), calls=%async_computation.2 | async-start | bytes 2097152 | tf_op jit(solution)/shard_map/all_to_all | solution.py:106
  20.3 22.5 %copy-start.6 = (u32[32]{0:T(128)S(1)}, u32[32]{0:T(128)}, u32[]{:S(2)}) copy-start(u32[32]{0:T(128)} %constant.136) | copy-start | bytes 388
  20.3 23.8 %copy-start.5 = (s32[8]{0:T(128)S(1)}, s32[8]{0:T(128)}, u32[]{:S(2)}) copy-start(s32[8]{0:T(128)} %param.12) | copy-start | bytes 100
  37.9 102.0 %all-to-all-start = ((bf16[16,16,8192]{2,1,0:T(8,128)(2,1)}), bf16[16,16,8192]{2,1,0:T(8,128)(2,1)}, u32[]{:S(2)}, u32[]{:S(2)}) async-start(bf16[16,16,8192]{2,1,0:T(8,128)(2,1)} %broadcast_select_fusion), calls=%async_computation | async-start | bytes 8388608 | tf_op jit(solution)/shard_map/all_to_all | solution.py:105
  139.9 32.4 %all-to-all-start.3 = ((bf16[128,16,256]{2,0,1:T(8,128)(2,1)}), bf16[128,16,256]{2,0,1:T(8,128)(2,1)S(1)}, u32[]{:S(2)}, u32[]{:S(2)}) async-start(bf16[128,16,256]{2,0,1:T(8,128)(2,1)} %all_to_all.55), calls=%async_computation.3 | async-start | bytes 2097152 | tf_op jit(solution)/shard_map/all_to_all | solution.py:119
  151.1 26.1 %copy-start.2 = (s32[2048]{0:T(1024)S(1)}, s32[2048]{0:T(1024)}, u32[]{:S(2)}) copy-start(s32[2048]{0:T(1024)} %param.13) | copy-start | bytes 24580
  172.3 52.5 %all-to-all-start.1 = ((bf16[128,16,512]{2,0,1:T(8,128)(2,1)}), bf16[128,16,512]{2,0,1:T(8,128)(2,1)}, u32[]{:S(2)}, u32[]{:S(2)}) async-start(bf16[128,16,512]{2,0,1:T(8,128)(2,1)} %copy.19), calls=%async_computation.1 | async-start | bytes 4194304 | tf_op jit(solution)/shard_map/all_to_all | solution.py:118
  317.9 5.0 %copy-start.4 = (s32[8]{0:T(128)S(1)}, s32[8]{0:T(128)}, u32[]{:S(2)}) copy-start(s32[8]{0:T(128)} %get-tuple-element.290) | copy-start | bytes 100
  317.9 52.4 %all-to-all-start.4 = ((bf16[16,128,512]{2,1,0:T(8,128)(2,1)}), bf16[16,128,512]{2,1,0:T(8,128)(2,1)S(1)}, u32[]{:S(2)}, u32[]{:S(2)}) async-start(bf16[16,128,512]{2,1,0:T(8,128)(2,1)} %bitcast.72), calls=%async_computation.4 | async-start | bytes 4194304 | tf_op jit(solution)/shard_map/all_to_all | solution.py:122
  383.0 5.1 %copy-start.3 = (s32[8]{0:T(128)S(1)}, s32[8]{0:T(128)}, u32[]{:S(2)}) copy-start(s32[8]{0:T(128)} %get-tuple-element.287) | copy-start | bytes 100
  383.0 97.5 %all-to-all-start.5 = ((bf16[16,16,8192]{2,1,0:T(8,128)(2,1)}), bf16[16,16,8192]{2,1,0:T(8,128)(2,1)}, u32[]{:S(2)}, u32[]{:S(2)}) async-start(bf16[16,16,8192]{2,1,0:T(8,128)(2,1)} %broadcast_select_fusion.1), calls=%async_computation.5 | async-start | bytes 8388608 | tf_op jit(solution)/shard_map/all_to_all | solution.py:124
  388.0 96.7 %copy-start.1 = (bf16[128,8192]{1,0:T(8,128)(2,1)S(1)}, bf16[128,8192]{1,0:T(8,128)(2,1)}, u32[]{:S(2)}) copy-start(bf16[128,8192]{1,0:T(8,128)(2,1)} %param.9) | copy-start | bytes 6291460
where the time goes:
time: 486 us; the launch traced here: 485 us
  waiting for transfers between devices  222 us (46%)
  blocking collectives  88.9 us (18%)
  local copies, waits for them, and re-layouts  52.8 us (11%)
  other arithmetic  38.8 us (8%)
  starting transfers between devices  34 us (7%)
  matrix products  31.6 us (7%)
  loops' own time  15.9 us (3%)
    all_to_all x1, waiting for transfers between devices, body(): lax.all_to_all(going_back, 'seq', split_axis=0, concat_axis=0, tiled=True)  92.4 us
    unnamed x1, blocking collectives  88.9 us
    all_to_all x1, waiting for transfers between devices, body(): lax.all_to_all(attended, 'seq', split_axis=0, concat_axis=1, tiled=True)  47.2 us
    all_to_all x1, waiting for transfers between devices, body(): lax.all_to_all(ready_queries, 'seq', split_axis=1, concat_axis=0, tiled=T...  45.9 us
    reduce_sum x10, other arithmetic, key_step(): totals = totals * factor + jnp.sum(weights.astype(jnp.float32), axis=1)  20.9 us
    dot_general x10, matrix products, key_step(): jnp.einsum('qd,kd->qk', query_block, key_block, preferred_element_type=jn...  20.6 us
    all_to_all x1, waiting for transfers between devices, body(): lax.all_to_all(spread, 'seq', split_axis=1, concat_axis=0, tiled=True)  18.7 us
    all_to_all x1, waiting for transfers between devices, body(): lax.all_to_all(outgoing[1], 'seq', split_axis=0, concat_axis=0, tiled=True)  17.6 us
  transfers between devices with their start and end apart: 6, of which 5 were waited for; matrix products, arithmetic and copies ran while one was open for 4% of the time, Pallas kernels for 0%

commit v1 on v0

v1 whole, which is shorter than its diff:
```python
import functools

import jax
import jax.numpy as jnp
from jax import lax
from jax.experimental import pallas as pl
from jax.experimental.pallas import tpu as pltpu
from jax.sharding import PartitionSpec as P

KVH = 8
HD = 128
masked_floor = -1e30
log2_e = 1.4426950408889634


def attend_kernel(block_rows, q_ref, k_ref, v_ref, key_blocks_ref, own_places_ref, segments_ref, o_ref, bias_ref):
    rows = q_ref.shape[0]
    total = k_ref.shape[0]
    heads = q_ref.shape[1] // HD

    @pl.when(pl.program_id(0) == 0)
    def _():
        own = own_places_ref[...]
        segments = segments_ref[...]
        places = lax.broadcasted_iota(jnp.int32, (rows, total), 1)
        mine = jnp.sum(jnp.where(places == own, segments, 0), axis=1, keepdims=True)
        first = jnp.sum(jnp.where(segments < mine, 1, 0), axis=1, keepdims=True)
        key_places = key_blocks_ref[...]
        allowed = (key_places >= first) & (key_places <= own)
        bias_ref[...] = jnp.where(allowed, 0.0, masked_floor).astype(jnp.float32)

    keys = k_ref[...]
    values = jnp.concatenate([v_ref[...], jnp.ones_like(v_ref)], axis=1)
    factor = (HD ** -0.5) * log2_e
    for head in range(heads):
        columns = pl.ds(head * HD, HD)
        scores = lax.dot_general(
            q_ref[:, columns], keys, (((1,), (1,)), ((), ())), preferred_element_type=jnp.float32
        )
        scores = scores + bias_ref[...]
        highest = jnp.max(scores, axis=1, keepdims=True)
        weights = jnp.exp2((scores - highest) * factor).astype(jnp.bfloat16)
        mixed = jnp.dot(weights, values, preferred_element_type=jnp.float32)
        o_ref[:, columns] = (mixed[:, :HD] / mixed[:, HD:]).astype(o_ref.dtype)


def attend(queries, all_keys, all_values, key_places, own_places, segments, block_rows):
    rows, width = queries.shape
    total = all_keys.shape[0]
    group = width // KVH
    whole = lambda i: (0, 0)
    return pl.pallas_call(
        functools.partial(attend_kernel, block_rows),
        grid=(KVH,),
        out_shape=jax.ShapeDtypeStruct((rows, width), jnp.bfloat16),
        in_specs=[
            pl.BlockSpec((rows, group), lambda i: (0, i)),
            pl.BlockSpec((total, HD), lambda i: (0, i)),
            pl.BlockSpec((total, HD), lambda i: (0, i)),
            pl.BlockSpec((1, total), whole),
            pl.BlockSpec((rows, 1), whole),
            pl.BlockSpec((1, total), whole),
        ],
        out_specs=pl.BlockSpec((rows, group), lambda i: (0, i)),
        scratch_shapes=[pltpu.VMEM((rows, total), jnp.float32)],
        compiler_params=pltpu.CompilerParams(vmem_limit_bytes=56 * 1024 * 1024),
    )(queries, all_keys, all_values, key_places, own_places, segments)


def body(queries, keys, values, stream_block, segment_ids):
    rows = queries.shape[0]
    block_rows = rows // stream_block.shape[0]
    inside = jnp.arange(block_rows, dtype=jnp.int32)
    own = (stream_block[:, None] * block_rows + inside[None, :]).reshape(-1)
    key_places = lax.all_gather(own, "seq", axis=0, tiled=True)
    all_keys = lax.all_gather(keys, "seq", axis=0, tiled=True)
    all_values = lax.all_gather(values, "seq", axis=0, tiled=True)
    return attend(
        queries, all_keys, all_values, key_places[None, :], own[:, None], segment_ids[None, :], block_rows
    )


def solution(mesh):
    placed = (
        P(("parts", "seq"), None),
        P(("parts", "seq"), None),
        P(("parts", "seq"), None),
        P(("parts", "seq")),
        P("parts"),
    )
    return jax.shard_map(
        body, mesh=mesh, in_specs=placed, out_specs=P(("parts", "seq"), None), check_vma=False
    )
```

time: 486 us -> 149 us (0.31)
  the two profiles are of different devices: /device:TPU:13 before, /device:TPU:0 now
where the time goes in v1:
time: 149 us
  waiting for transfers between devices  82.6 us (55%)
  Pallas kernels  27.8 us (19%)
  blocking collectives  23.3 us (16%)
  between operations  13.4 us (9%)
    all_gather x1, waiting for transfers between devices, body(): all_values = lax.all_gather(values, 'seq', axis=0, tiled=True)  51.2 us
    all_gather x1, waiting for transfers between devices, body(): all_keys = lax.all_gather(keys, 'seq', axis=0, tiled=True)  29.9 us
    pallas_call x1, Pallas kernels, attend(): pl.pallas_call(functools.partial(attend_kernel, block_rows), grid=(KVH,),...  27.8 us
    all_gather x1, blocking collectives, body(): key_places = lax.all_gather(own, 'seq', axis=0, tiled=True)  23.3 us
  transfers between devices with their start and end apart: 2, of which 2 were waited for; matrix products, arithmetic and copies ran while one was open for 1% of the time, Pallas kernels for 0%

profile of v1, /device:TPU:0, one launch (start us, length us, event | category | flops | bytes accessed | tf_op | source)
XLA Modules:
  0.0 148.7 jit_solution(1108796062103481519)
XLA Ops:
  6.5 0.0 all-gather.4.cloned.1.call-start
  6.5 0.7 all-gather.4.cloned.1.call-update
  7.3 0.0 all-gather.6.cloned.1.call-start
  7.3 0.7 all-gather.6.cloned.1.call-update
  8.0 0.7 broadcast_multiply_fusion
  8.7 0.1 iota_add_fusion
  8.7 0.1 reshape.28
  8.8 0.7 add.32.own_places_ref
  9.5 23.3 %all-gather = s32[16,1,128]{2,1,0:T(1,128)} all-gather(s32[1,1,128]{2,1,0:T(1,128)S(1)} %reshape.28), channel_id=1, replica_groups=mesh['parts'=2,'seq'=16] {'seq'}, dimensions={0}, use_global_device_ids=true | all-gather | bytes 8704 | tf_op jit(solution)/shard_map/all_gather | solution.py:75
  32.9 29.9 %all-gather.4.cloned.1.call-done.k_ref = bf16[2048,1024]{1,0:T(8,128)(2,1)} async-done(((bf16[128,1024]{1,0:T(8,128)(2,1)}), bf16[2048,1024]{1,0:T(8,128)(2,1)}) %all-gather.4.cloned.1.call-update) | async-done | bytes 4194320 | tf_op jit(solution)/shard_map/all_gather | solution.py:76
  62.8 51.2 %all-gather.6.cloned.1.call-done.v_ref = bf16[2048,1024]{1,0:T(8,128)(2,1)} async-done(((bf16[128,1024]{1,0:T(8,128)(2,1)}), bf16[2048,1024]{1,0:T(8,128)(2,1)}) %all-gather.6.cloned.1.call-update) | async-done | bytes 4194320 | tf_op jit(solution)/shard_map/all_gather | solution.py:77
  114.1 27.8 %shard_map.55 = bf16[128,8192]{1,0:T(8,128)(2,1)} custom-call(bf16[128,8192]{1,0:T(8,128)(2,1)} %q_ref.1, bf16[2048,1024]{1,0:T(8,128)(2,1)} %all-gather.4.cloned.1.call-done.k_ref, bf16[2048,1024]{1,0:T(8,128)(2,1)} %all-gather.6.cloned.1.call-done.v_ref, s32[1,2048]{1,0:T(1,128)} %bitcast.2, s32[128,1]{1,0:T(8,128)} %add.32.own_places_ref, s32[1,2048]{1,0:T(1,128)} %bitcast.3), custom_call_target="tpu_custom_call" | custom-call | tf_op jit(solution)/shard_map/pallas_call | solution.py:52
Async XLA Ops:
  6.5 56.3 %all-gather.4.cloned.1.call-start = ((), (), s32[]{:S(2)}) async-start(), calls=%async_computation | async-start | bytes 4456448 | tf_op jit(solution)/shard_map/all_gather | solution.py:76
  7.3 106.8 %all-gather.6.cloned.1.call-start = ((), (), s32[]{:S(2)}) async-start(), calls=%async_computation.1 | async-start | bytes 4456448 | tf_op jit(solution)/shard_map/all_gather | solution.py:77
Sparse Core Ops, SparseCore 0:
  9.5 53.2 all-gather.3
  65.0 49.0 all-gather.5

commit v2 on v1

v2 whole, which is shorter than its diff:
```python
import functools

import jax
import jax.numpy as jnp
from jax import lax
from jax.experimental import pallas as pl
from jax.experimental.pallas import tpu as pltpu
from jax.sharding import PartitionSpec as P

KVH = 8
HD = 128
masked_floor = -1e30
log2_e = 1.4426950408889634
factor = (HD ** -0.5) * log2_e

RK, RP, RV, LK, LP, LV, SK0, SP0, SV0, SK1, SP1, SV1 = range(12)


def ring_attend_kernel(
    chips, depth, q_ref, k_ref, v_ref, places_ref, own_ref, segments_ref, o_ref,
    k_buf, v_buf, p_buf, bias_ref, first_ref, acc_ref, sum_ref, top_ref, send_sem, recv_sem,
):
    rows = q_ref.shape[0]
    heads = q_ref.shape[1] // (KVH * HD)
    half = chips // 2

    me = lax.axis_index("seq")
    core = me % 2
    chip = me // 2
    columns = chips // depth
    z = chip // columns
    y = chip % columns
    place = z + y * (2 * depth - 1 - 2 * z)

    def device_at(ring_place):
        turn = ring_place // depth
        step = ring_place % depth
        return ((step + turn * (depth - 1 - 2 * step)) * columns + turn) * 2 + core

    right = device_at((place + 1) % chips)
    left = device_at((place + chips - 1) % chips)
    sibling = chip * 2 + 1 - core

    barrier = pltpu.get_barrier_semaphore()
    for peer in (right, left, sibling):
        pl.semaphore_signal(barrier, inc=1, device_id={"seq": peer}, device_id_type=pl.DeviceIdType.MESH)

    def part(buf, slot, quarter):
        if buf is p_buf:
            return p_buf.at[slot, quarter]
        return buf.at[slot, pl.ds(quarter * rows, rows)]

    def copy(kind, buf, source, target, peer):
        return pltpu.make_async_remote_copy(
            src_ref=part(buf, *source),
            dst_ref=part(buf, *target),
            send_sem=send_sem.at[kind, target[0]],
            recv_sem=recv_sem.at[kind, target[0]],
            device_id={"seq": peer},
            device_id_type=pl.DeviceIdType.MESH,
        )

    def follow(slot, quarter, last, buf):
        which = 0 if buf is k_buf else 1 if buf is p_buf else 2
        origin = isinstance(slot, int) and slot == 0
        final = isinstance(slot, int) and slot == half
        out = []
        if not final:
            if quarter == 0 and (buf is not v_buf or not last):
                out.append(((RK, RP, RV)[which], buf, (slot, 0), (slot + 1, 0), right))
            if (quarter == 1 or origin) and (buf is v_buf or not last):
                out.append(((LK, LP, LV)[which], buf, (slot, quarter), (slot + 1, 0 if last else 1), left))
        if origin or final:
            out.append(((SK0, SP0, SV0)[which], buf, (slot, 0), (slot, 1), sibling))
        else:
            kinds = (SK0, SP0, SV0) if quarter == 0 else (SK1, SP1, SV1)
            out.append((kinds[which], buf, (slot, quarter), (slot, quarter + 2), sibling))
        return out

    def wait_for(kind, buf, slot, quarter):
        copy(kind, buf, (slot, quarter), (slot, quarter), sibling).wait_recv()

    def arrive(slot, last):
        for buf, right_kind, left_kind in ((k_buf, RK, LK), (p_buf, RP, LP), (v_buf, RV, LV)):
            for kind, quarter in ((right_kind, 0), (left_kind, 1)):
                wait_for(kind, buf, slot, quarter)
                for item in follow(slot, quarter, last, buf):
                    copy(*item).start()
        for buf, kinds in ((k_buf, (SK0, SK1)), (p_buf, (SP0, SP1)), (v_buf, (SV0, SV1))):
            wait_for(kinds[0], buf, slot, 2)
            wait_for(kinds[1], buf, slot, 3)

    def sent(slot, quarters, last):
        for buf in (k_buf, p_buf, v_buf):
            for quarter in quarters:
                for item in follow(slot, quarter, last, buf):
                    copy(*item).wait_send()

    def compute(slot, parts, opening, closing):
        width = parts * rows
        key_places = jnp.concatenate([p_buf[slot, n][0:1, :] for n in range(parts)], axis=1)
        allowed = (key_places >= first_ref[...]) & (key_places <= own_ref[...])
        bias_ref[:, 0:width] = jnp.where(allowed, 0.0, masked_floor).astype(jnp.float32)

        def key_head(index, carry):
            columns = pl.ds(pl.multiple_of(index * HD, HD), HD)
            keys = k_buf[slot, 0:width, columns]
            values = v_buf[slot, 0:width, columns]
            values = jnp.concatenate([values, jnp.ones_like(values)], axis=1)
            for head in range(heads):
                here = pl.ds(pl.multiple_of((index * heads + head) * HD, HD), HD)
                scores = lax.dot_general(
                    q_ref[:, here], keys, (((1,), (1,)), ((), ())), preferred_element_type=jnp.float32
                )
                scores = scores + bias_ref[:, 0:width]
                highest = jnp.max(scores, axis=1, keepdims=True)
                if opening:
                    top = jnp.broadcast_to(highest, (rows, HD))
                else:
                    before = top_ref[:, here]
                    top = jnp.maximum(before, highest)
                wide = jnp.concatenate([top] * (width // HD), axis=1)
                weights = jnp.exp2((scores - wide) * factor).astype(jnp.bfloat16)
                mixed = jnp.dot(weights, values, preferred_element_type=jnp.float32)
                acc, total = mixed[:, :HD], mixed[:, HD:]
                if not opening:
                    shrink = jnp.exp2((before - top) * factor)
                    acc = acc_ref[:, here] * shrink + acc
                    total = sum_ref[:, here] * shrink + total
                if closing:
                    o_ref[:, here] = (acc / total).astype(o_ref.dtype)
                else:
                    acc_ref[:, here] = acc
                    sum_ref[:, here] = total
                    top_ref[:, here] = top
            return carry

        lax.fori_loop(0, KVH, key_head, 0)

    k_buf[0, 0:rows, :] = k_ref[...]
    v_buf[0, 0:rows, :] = v_ref[...]
    p_buf[0, 0] = places_ref[...]
    pl.semaphore_wait(barrier, 3)
    for buf in (k_buf, p_buf, v_buf):
        for item in follow(0, 0, False, buf):
            copy(*item).start()

    own = own_ref[...]
    segments = segments_ref[...]
    spots = lax.broadcasted_iota(jnp.int32, (rows, segments.shape[1]), 1)
    mine = jnp.sum(jnp.where(spots == own, segments, 0), axis=1, keepdims=True)
    first_ref[...] = jnp.sum(jnp.where(segments < mine, 1, 0), axis=1, keepdims=True)

    wait_for(SK0, k_buf, 0, 1)
    wait_for(SP0, p_buf, 0, 1)
    wait_for(SV0, v_buf, 0, 1)
    compute(0, 2, True, False)

    def middle(slot, carry):
        arrive(slot, False)
        compute(slot, 4, False, False)
        return carry

    lax.fori_loop(1, half - 1, middle, 0)
    arrive(half - 1, True)
    compute(half - 1, 4, False, False)

    for buf, kind in ((k_buf, RK), (p_buf, RP), (v_buf, LV)):
        wait_for(kind, buf, half, 0)
        for item in follow(half, 0, False, buf):
            copy(*item).start()
    wait_for(SK0, k_buf, half, 1)
    wait_for(SP0, p_buf, half, 1)
    wait_for(SV0, v_buf, half, 1)
    compute(half, 2, False, True)

    sent(0, (0,), False)

    def settle(slot, carry):
        sent(slot, (0, 1), False)
        return carry

    lax.fori_loop(1, half - 1, settle, 0)
    sent(half - 1, (0, 1), True)
    sent(half, (0,), False)


def ring_attend(queries, keys, values, places, own_places, segments, chips, depth):
    rows, width = queries.shape
    slots = chips // 2 + 1
    vmem = pl.BlockSpec(memory_space=pltpu.VMEM)
    return pl.pallas_call(
        functools.partial(ring_attend_kernel, chips, depth),
        out_shape=jax.ShapeDtypeStruct((rows, width), jnp.bfloat16),
        in_specs=[vmem] * 6,
        out_specs=vmem,
        scratch_shapes=[
            pltpu.VMEM((slots, 4 * rows, keys.shape[1]), jnp.bfloat16),
            pltpu.VMEM((slots, 4 * rows, keys.shape[1]), jnp.bfloat16),
            pltpu.VMEM((slots, 4, 8, rows), jnp.int32),
            pltpu.VMEM((rows, 4 * rows), jnp.float32),
            pltpu.VMEM((rows, 1), jnp.int32),
            pltpu.VMEM((rows, width), jnp.float32),
            pltpu.VMEM((rows, width), jnp.float32),
            pltpu.VMEM((rows, width), jnp.float32),
            pltpu.SemaphoreType.DMA((12, slots)),
            pltpu.SemaphoreType.DMA((12, slots)),
        ],
        compiler_params=pltpu.CompilerParams(
            collective_id=0, has_side_effects=True, vmem_limit_bytes=60 * 1024 * 1024
        ),
    )(queries, keys, values, places, own_places, segments)


def body(queries, keys, values, stream_block, segment_ids):
    rows = queries.shape[0]
    block_rows = rows // stream_block.shape[0]
    inside = jnp.arange(block_rows, dtype=jnp.int32)
    own = (stream_block[:, None] * block_rows + inside[None, :]).reshape(-1)
    chips = lax.axis_size("seq") // 2
    depth = chips // 2 if lax.axis_size("parts") == 2 else chips
    places = jnp.broadcast_to(own[None, :], (8, rows))
    return ring_attend(
        queries, keys, values, places, own[:, None], segment_ids[None, :], chips, depth
    )


def solution(mesh):
    placed = (
        P(("parts", "seq"), None),
        P(("parts", "seq"), None),
        P(("parts", "seq"), None),
        P(("parts", "seq")),
        P("parts"),
    )
    return jax.shard_map(
        body, mesh=mesh, in_specs=placed, out_specs=P(("parts", "seq"), None), check_vma=False
    )
```

time: 149 us -> 67.3 us (0.45)
  waiting for transfers between devices: 82.6 us -> 0 us
  Pallas kernels: 27.8 us -> 61.7 us
  blocking collectives: 23.3 us -> 0 us
  between operations: 13.4 us -> 0.01 us
  local copies, waits for them, and re-layouts: 0.79 us -> 4.49 us
    all_gather x2 -> x0, waiting for transfers between devices: 81.2 us -> none  [the longest x1 51.2 us: body(): all_values = lax.all_gather(values, 'seq', axis=0, tiled=True)]
    pallas_call x1, Pallas kernels: 27.8 us -> 61.7 us  [ring_attend(): pl.pallas_call(functools.partial(ring_attend_kernel, chips, depth), out_s...]
    all_gather x1 -> x0, blocking collectives: 23.3 us -> none  [body(): key_places = lax.all_gather(own, 'seq', axis=0, tiled=True)]
    unnamed x1, local copies, waits for them, and re-layouts: 0.08 us -> 3.1 us
  transfers between devices with their start and end apart: 2 -> 0, of which waited for: 2 -> 0; matrix products, arithmetic and copies ran while one was open for 1% -> 0% of each run, Pallas kernels for 0% -> 0%
where the time goes in v2:
time: 67.3 us; the launch traced here: 67 us
  Pallas kernels  61.7 us (92%)
  local copies, waits for them, and re-layouts  4.49 us (7%)
  other arithmetic  0.73 us (1%)
    pallas_call x1, Pallas kernels, ring_attend(): pl.pallas_call(functools.partial(ring_attend_kernel, chips, depth), out_s...  61.7 us
    unnamed x1, local copies, waits for them, and re-layouts  3.1 us

profile of v2, /device:TPU:0, one launch (start us, length us, event | category | flops | bytes accessed | tf_op | source)
XLA Modules:
  0.0 67.0 jit_solution(4167546224927183055)
XLA Ops:
  0.0 0.7 broadcast_multiply_fusion
  0.7 0.1 iota_add_fusion
  0.7 0.1 add.33
  0.8 0.6 broadcast_in_dim.4.places_ref
  1.4 0.7 %add.35.own_ref = s32[128,1]{1,0:T(8,128)} reshape(s32[8,16]{1,0:T(8,128)S(1)} %iota_add_fusion) | data formatting | bytes 1024 | tf_op jit(solution)/shard_map/add | solution.py:219
  2.1 61.7 %shard_map.55 = bf16[128,8192]{1,0:T(8,128)(2,1)} custom-call(bf16[128,8192]{1,0:T(8,128)(2,1)} %q_ref.1, bf16[128,1024]{1,0:T(8,128)(2,1)} %k_ref.1, bf16[128,1024]{1,0:T(8,128)(2,1)} %v_ref.1, s32[8,128]{1,0:T(8,128)} %broadcast_in_dim.4.places_ref, s32[128,1]{1,0:T(8,128)} %add.35.own_ref, s32[1,2048]{1,0:T(1,128)} %bitcast.1), custom_call_target="tpu_custom_call" | custom-call | tf_op jit(solution)/shard_map/pallas_call | solution.py:192
  63.9 3.1 %copy.8 = bf16[128,8192]{1,0:T(8,128)(2,1)} copy(bf16[128,8192]{1,0:T(8,128)(2,1)} %shard_map.55) | data formatting | bytes 4194304

commit v3 on v2

--- a/solution.py
+++ b/solution.py
@@ -17,7 +17,7 @@
 
 
 def ring_attend_kernel(
-    chips, depth, q_ref, k_ref, v_ref, places_ref, own_ref, segments_ref, o_ref,
+    chips, depth, q_ref, k_ref, v_ref, blocks_ref, segments_ref, o_ref,
     k_buf, v_buf, p_buf, bias_ref, first_ref, acc_ref, sum_ref, top_ref, send_sem, recv_sem,
 ):
     rows = q_ref.shape[0]
@@ -98,58 +98,73 @@
 
     def compute(slot, parts, opening, closing):
         width = parts * rows
-        key_places = jnp.concatenate([p_buf[slot, n][0:1, :] for n in range(parts)], axis=1)
-        allowed = (key_places >= first_ref[...]) & (key_places <= own_ref[...])
-        bias_ref[:, 0:width] = jnp.where(allowed, 0.0, masked_floor).astype(jnp.float32)
+        for n in range(parts):
+            key_places = jnp.transpose(jnp.broadcast_to(p_buf[slot, n][0:1, :], (rows, rows)))
+            allowed = (key_places >= first_ref[0:1, :]) & (key_places <= p_buf[0, 0][0:1, :])
+            bias_ref[n * rows : (n + 1) * rows, :] = jnp.where(allowed, 0.0, masked_floor).astype(jnp.float32)
 
         def key_head(index, carry):
             columns = pl.ds(pl.multiple_of(index * HD, HD), HD)
             keys = k_buf[slot, 0:width, columns]
-            values = v_buf[slot, 0:width, columns]
-            values = jnp.concatenate([values, jnp.ones_like(values)], axis=1)
-            for head in range(heads):
-                here = pl.ds(pl.multiple_of((index * heads + head) * HD, HD), HD)
+            values = jnp.transpose(v_buf[slot, 0:width, columns])
+            values = jnp.concatenate([values, jnp.ones((16, width), jnp.bfloat16)], axis=0)
+            for n in range(heads // 2):
+                pair = index * (heads // 2) + n
+                one = pl.ds(pl.multiple_of(pair * 2 * HD, HD), HD)
+                two = pl.ds(pl.multiple_of(pair * 2 * HD + HD, HD), HD)
+                asked = jnp.concatenate([q_ref[:, one], q_ref[:, two]], axis=0)
                 scores = lax.dot_general(
-                    q_ref[:, here], keys, (((1,), (1,)), ((), ())), preferred_element_type=jnp.float32
+                    keys, asked, (((1,), (1,)), ((), ())), preferred_element_type=jnp.float32
                 )
-                scores = scores + bias_ref[:, 0:width]
-                highest = jnp.max(scores, axis=1, keepdims=True)
-                if opening:
-                    top = jnp.broadcast_to(highest, (rows, HD))
-                else:
-                    before = top_ref[:, here]
-                    top = jnp.maximum(before, highest)
-                wide = jnp.concatenate([top] * (width // HD), axis=1)
-                weights = jnp.exp2((scores - wide) * factor).astype(jnp.bfloat16)
-                mixed = jnp.dot(weights, values, preferred_element_type=jnp.float32)
-                acc, total = mixed[:, :HD], mixed[:, HD:]
+                bias = bias_ref[0:width, :]
+                scores = scores + jnp.concatenate([bias, bias], axis=1)
+                top = jnp.max(scores, axis=0, keepdims=True)
+                if not opening:
+                    before = top_ref[pair]
+                    top = jnp.maximum(before, top)
+                weights = jnp.exp2((scores - top) * factor).astype(jnp.bfloat16)
+                mixed = jnp.dot(values, weights, preferred_element_type=jnp.float32)
+                acc, total = mixed[:HD, :], mixed[HD : HD + 1, :]
                 if not opening:
                     shrink = jnp.exp2((before - top) * factor)
-                    acc = acc_ref[:, here] * shrink + acc
-                    total = sum_ref[:, here] * shrink + total
+                    acc = acc_ref[pair] * shrink + acc
+                    total = sum_ref[pair] * shrink + total
                 if closing:
-                    o_ref[:, here] = (acc / total).astype(o_ref.dtype)
+                    done = (acc / total).astype(o_ref.dtype)
+                    o_ref[:, one] = jnp.transpose(done[:, :rows])
+                    o_ref[:, two] = jnp.transpose(done[:, rows:])
                 else:
-                    acc_ref[:, here] = acc
-                    sum_ref[:, here] = total
-                    top_ref[:, here] = top
+                    acc_ref[pair] = acc
+                    sum_ref[pair] = total
+                    top_ref[pair] = top
             return carry
 
         lax.fori_loop(0, KVH, key_head, 0)
 
     k_buf[0, 0:rows, :] = k_ref[...]
     v_buf[0, 0:rows, :] = v_ref[...]
-    p_buf[0, 0] = places_ref[...]
+    blocks = blocks_ref.shape[0]
+    block_rows = rows // blocks
+    lane = lax.broadcasted_iota(jnp.int32, (8, rows), 1)
+    where_from = lane * 0
+    for n in range(blocks):
+        where_from = jnp.where(
+            (lane >= n * block_rows) & (lane < (n + 1) * block_rows),
+            lane + (blocks_ref[n] - n) * block_rows,
+            where_from,
+        )
+    p_buf[0, 0] = where_from
     pl.semaphore_wait(barrier, 3)
     for buf in (k_buf, p_buf, v_buf):
         for item in follow(0, 0, False, buf):
             copy(*item).start()
 
-    own = own_ref[...]
+    own = jnp.transpose(jnp.broadcast_to(where_from[0:1, :], (rows, rows)))[:, 0:1]
     segments = segments_ref[...]
     spots = lax.broadcasted_iota(jnp.int32, (rows, segments.shape[1]), 1)
     mine = jnp.sum(jnp.where(spots == own, segments, 0), axis=1, keepdims=True)
-    first_ref[...] = jnp.sum(jnp.where(segments < mine, 1, 0), axis=1, keepdims=True)
+    first = jnp.sum(jnp.where(segments < mine, 1, 0), axis=1, keepdims=True)
+    first_ref[...] = jnp.transpose(jnp.broadcast_to(first, (rows, rows)))[0:8, :]
 
     wait_for(SK0, k_buf, 0, 1)
     wait_for(SP0, p_buf, 0, 1)
@@ -185,43 +200,38 @@
     sent(half, (0,), False)
 
 
-def ring_attend(queries, keys, values, places, own_places, segments, chips, depth):
+def ring_attend(queries, keys, values, blocks, segments, chips, depth):
     rows, width = queries.shape
     slots = chips // 2 + 1
     vmem = pl.BlockSpec(memory_space=pltpu.VMEM)
     return pl.pallas_call(
         functools.partial(ring_attend_kernel, chips, depth),
         out_shape=jax.ShapeDtypeStruct((rows, width), jnp.bfloat16),
-        in_specs=[vmem] * 6,
+        in_specs=[vmem] * 3 + [pl.BlockSpec(memory_space=pltpu.SMEM), vmem],
         out_specs=vmem,
         scratch_shapes=[
             pltpu.VMEM((slots, 4 * rows, keys.shape[1]), jnp.bfloat16),
             pltpu.VMEM((slots, 4 * rows, keys.shape[1]), jnp.bfloat16),
             pltpu.VMEM((slots, 4, 8, rows), jnp.int32),
-            pltpu.VMEM((rows, 4 * rows), jnp.float32),
-            pltpu.VMEM((rows, 1), jnp.int32),
-            pltpu.VMEM((rows, width), jnp.float32),
-            pltpu.VMEM((rows, width), jnp.float32),
-            pltpu.VMEM((rows, width), jnp.float32),
+            pltpu.VMEM((4 * rows, rows), jnp.float32),
+            pltpu.VMEM((8, rows), jnp.int32),
+            pltpu.VMEM((width // (2 * HD), HD, 2 * rows), jnp.float32),
+            pltpu.VMEM((width // (2 * HD), 1, 2 * rows), jnp.float32),
+            pltpu.VMEM((width // (2 * HD), 1, 2 * rows), jnp.float32),
             pltpu.SemaphoreType.DMA((12, slots)),
             pltpu.SemaphoreType.DMA((12, slots)),
         ],
         compiler_params=pltpu.CompilerParams(
             collective_id=0, has_side_effects=True, vmem_limit_bytes=60 * 1024 * 1024
         ),
-    )(queries, keys, values, places, own_places, segments)
+    )(queries, keys, values, blocks, segments)
 
 
 def body(queries, keys, values, stream_block, segment_ids):
-    rows = queries.shape[0]
-    block_rows = rows // stream_block.shape[0]
-    inside = jnp.arange(block_rows, dtype=jnp.int32)
-    own = (stream_block[:, None] * block_rows + inside[None, :]).reshape(-1)
     chips = lax.axis_size("seq") // 2
     depth = chips // 2 if lax.axis_size("parts") == 2 else chips
-    places = jnp.broadcast_to(own[None, :], (8, rows))
     return ring_attend(
-        queries, keys, values, places, own[:, None], segment_ids[None, :], chips, depth
+        queries, keys, values, stream_block, segment_ids[None, :], chips, depth
     )
 
 

time: 67.3 us -> 85 us (1.26)
  Pallas kernels: 61.7 us -> 81.7 us
  local copies, waits for them, and re-layouts: 4.49 us -> 3.1 us
    pallas_call x1, Pallas kernels: 61.7 us -> 81.7 us  [ring_attend(): pl.pallas_call(functools.partial(ring_attend_kernel, chips, depth), out_s...]
where the time goes in v3:
time: 85 us; the launch traced here: 84.8 us
  Pallas kernels  81.7 us (96%)
  local copies, waits for them, and re-layouts  3.1 us (4%)
    pallas_call x1, Pallas kernels, ring_attend(): pl.pallas_call(functools.partial(ring_attend_kernel, chips, depth), out_s...  81.7 us
    unnamed x1, local copies, waits for them, and re-layouts  3.1 us

profile of v3, /device:TPU:0, one launch (start us, length us, event | category | flops | bytes accessed | tf_op | source)
XLA Modules:
  0.0 84.8 jit_solution(14540835549489363829)
XLA Ops:
  0.0 81.7 %shard_map.55 = bf16[128,8192]{1,0:T(8,128)(2,1)} custom-call(bf16[128,8192]{1,0:T(8,128)(2,1)} %q_ref.1, bf16[128,1024]{1,0:T(8,128)(2,1)} %k_ref.1, bf16[128,1024]{1,0:T(8,128)(2,1)} %v_ref.1, s32[8]{0:T(128)} %blocks_ref.1, s32[1,2048]{1,0:T(1,128)} %bitcast.1), custom_call_target="tpu_custom_call" | custom-call | tf_op jit(solution)/shard_map/pallas_call | solution.py:207
  81.7 3.1 %copy.7 = bf16[128,8192]{1,0:T(8,128)(2,1)} copy(bf16[128,8192]{1,0:T(8,128)(2,1)} %shard_map.55) | data formatting | bytes 4194304

commit v4 on v3

--- a/solution.py
+++ b/solution.py
@@ -12,13 +12,14 @@
 masked_floor = -1e30
 log2_e = 1.4426950408889634
 factor = (HD ** -0.5) * log2_e
+together = 2
 
 RK, RP, RV, LK, LP, LV, SK0, SP0, SV0, SK1, SP1, SV1 = range(12)
 
 
 def ring_attend_kernel(
     chips, depth, q_ref, k_ref, v_ref, blocks_ref, segments_ref, o_ref,
-    k_buf, v_buf, p_buf, bias_ref, first_ref, acc_ref, sum_ref, top_ref, send_sem, recv_sem,
+    k_buf, v_buf, p_buf, bias_ref, first_ref, own_ref, acc_ref, sum_ref, top_ref, send_sem, recv_sem,
 ):
     rows = q_ref.shape[0]
     heads = q_ref.shape[1] // (KVH * HD)
@@ -80,15 +81,26 @@
     def wait_for(kind, buf, slot, quarter):
         copy(kind, buf, (slot, quarter), (slot, quarter), sibling).wait_recv()
 
-    def arrive(slot, last):
-        for buf, right_kind, left_kind in ((k_buf, RK, LK), (p_buf, RP, LP), (v_buf, RV, LV)):
+    def take(slot, last, entries):
+        for buf, right_kind, left_kind in entries:
             for kind, quarter in ((right_kind, 0), (left_kind, 1)):
                 wait_for(kind, buf, slot, quarter)
                 for item in follow(slot, quarter, last, buf):
                     copy(*item).start()
+
+    def arrive_keys(slot, last):
+        take(slot, last, ((k_buf, RK, LK), (p_buf, RP, LP)))
+
+    def arrive_values(slot, last):
+        take(slot, last, ((v_buf, RV, LV),))
         for buf, kinds in ((k_buf, (SK0, SK1)), (p_buf, (SP0, SP1)), (v_buf, (SV0, SV1))):
             wait_for(kinds[0], buf, slot, 2)
             wait_for(kinds[1], buf, slot, 3)
+
+    def arrive_last(buf, kind):
+        wait_for(kind, buf, half, 0)
+        for item in follow(half, 0, False, buf):
+            copy(*item).start()
 
     def sent(slot, quarters, last):
         for buf in (k_buf, p_buf, v_buf):
@@ -96,50 +108,57 @@
                 for item in follow(slot, quarter, last, buf):
                     copy(*item).wait_send()
 
-    def compute(slot, parts, opening, closing):
+    def compute(slot, parts, opening, closing, begin=0, end=KVH):
         width = parts * rows
-        for n in range(parts):
-            key_places = jnp.transpose(jnp.broadcast_to(p_buf[slot, n][0:1, :], (rows, rows)))
-            allowed = (key_places >= first_ref[0:1, :]) & (key_places <= p_buf[0, 0][0:1, :])
-            bias_ref[n * rows : (n + 1) * rows, :] = jnp.where(allowed, 0.0, masked_floor).astype(jnp.float32)
+        if begin == 0:
+            key_places = jnp.concatenate([p_buf[slot, n][0:1, :] for n in range(parts)], axis=1)
+            allowed = (key_places >= first_ref[...]) & (key_places <= own_ref[...])
+            bias_ref[:, 0:width] = jnp.where(allowed, 0.0, masked_floor).astype(jnp.float32)
 
         def key_head(index, carry):
             columns = pl.ds(pl.multiple_of(index * HD, HD), HD)
             keys = k_buf[slot, 0:width, columns]
-            values = jnp.transpose(v_buf[slot, 0:width, columns])
-            values = jnp.concatenate([values, jnp.ones((16, width), jnp.bfloat16)], axis=0)
-            for n in range(heads // 2):
-                pair = index * (heads // 2) + n
-                one = pl.ds(pl.multiple_of(pair * 2 * HD, HD), HD)
-                two = pl.ds(pl.multiple_of(pair * 2 * HD + HD, HD), HD)
-                asked = jnp.concatenate([q_ref[:, one], q_ref[:, two]], axis=0)
+            values = v_buf[slot, 0:width, columns]
+            values = jnp.concatenate([values, jnp.ones_like(values)], axis=1)
+            for start in range(0, heads, together):
+                spots = [
+                    pl.ds(pl.multiple_of((index * heads + start + n) * HD, HD), HD) for n in range(together)
+                ]
+                asked = jnp.concatenate([q_ref[:, spot] for spot in spots], axis=0)
                 scores = lax.dot_general(
-                    keys, asked, (((1,), (1,)), ((), ())), preferred_element_type=jnp.float32
+                    asked, keys, (((1,), (1,)), ((), ())), preferred_element_type=jnp.float32
                 )
-                bias = bias_ref[0:width, :]
-                scores = scores + jnp.concatenate([bias, bias], axis=1)
-                top = jnp.max(scores, axis=0, keepdims=True)
-                if not opening:
-                    before = top_ref[pair]
-                    top = jnp.maximum(before, top)
-                weights = jnp.exp2((scores - top) * factor).astype(jnp.bfloat16)
-                mixed = jnp.dot(values, weights, preferred_element_type=jnp.float32)
-                acc, total = mixed[:HD, :], mixed[HD : HD + 1, :]
-                if not opening:
-                    shrink = jnp.exp2((before - top) * factor)
-                    acc = acc_ref[pair] * shrink + acc
-                    total = sum_ref[pair] * shrink + total
-                if closing:
-                    done = (acc / total).astype(o_ref.dtype)
-                    o_ref[:, one] = jnp.transpose(done[:, :rows])
-                    o_ref[:, two] = jnp.transpose(done[:, rows:])
-                else:
-                    acc_ref[pair] = acc
-                    sum_ref[pair] = total
-                    top_ref[pair] = top
+                weights, olds, tops = [], [], []
+                for n, spot in enumerate(spots):
+                    mine = scores[n * rows : (n + 1) * rows] + bias_ref[:, 0:width]
+                    highest = jnp.max(mine, axis=1, keepdims=True)
+                    if opening:
+                        top = jnp.broadcast_to(highest, (rows, HD))
+                    else:
+                        olds.append(top_ref[:, spot])
+                        top = jnp.maximum(olds[n], highest)
+                    tops.append(top)
+                    wide = jnp.concatenate([top] * (width // HD), axis=1)
+                    weights.append(jnp.exp2((mine - wide) * factor).astype(jnp.bfloat16))
+                mixed = jnp.dot(
+                    jnp.concatenate(weights, axis=0), values, preferred_element_type=jnp.float32
+                )
+                for n, spot in enumerate(spots):
+                    acc = mixed[n * rows : (n + 1) * rows, :HD]
+                    total = mixed[n * rows : (n + 1) * rows, HD:]
+                    if not opening:
+                        shrink = jnp.exp2((olds[n] - tops[n]) * factor)
+                        acc = acc_ref[:, spot] * shrink + acc
+                        total = sum_ref[:, spot] * shrink + total
+                    if closing:
+                        o_ref[:, spot] = (acc / total).astype(o_ref.dtype)
+                    else:
+                        acc_ref[:, spot] = acc
+                        sum_ref[:, spot] = total
+                        top_ref[:, spot] = tops[n]
             return carry
 
-        lax.fori_loop(0, KVH, key_head, 0)
+        lax.fori_loop(begin, end, key_head, 0)
 
     k_buf[0, 0:rows, :] = k_ref[...]
     v_buf[0, 0:rows, :] = v_ref[...]
@@ -163,27 +182,34 @@
     segments = segments_ref[...]
     spots = lax.broadcasted_iota(jnp.int32, (rows, segments.shape[1]), 1)
     mine = jnp.sum(jnp.where(spots == own, segments, 0), axis=1, keepdims=True)
-    first = jnp.sum(jnp.where(segments < mine, 1, 0), axis=1, keepdims=True)
-    first_ref[...] = jnp.transpose(jnp.broadcast_to(first, (rows, rows)))[0:8, :]
+    first_ref[...] = jnp.sum(jnp.where(segments < mine, 1, 0), axis=1, keepdims=True)
+    own_ref[...] = own
 
     wait_for(SK0, k_buf, 0, 1)
     wait_for(SP0, p_buf, 0, 1)
     wait_for(SV0, v_buf, 0, 1)
     compute(0, 2, True, False)
+    arrive_keys(1, False)
+    arrive_values(1, False)
+
+    def advance(slot, last):
+        compute(slot, 4, False, False, 0, KVH // 2)
+        arrive_keys(slot + 1, last)
+        compute(slot, 4, False, False, KVH // 2, KVH)
+        arrive_values(slot + 1, last)
 
     def middle(slot, carry):
-        arrive(slot, False)
-        compute(slot, 4, False, False)
+        advance(slot, False)
         return carry
 
-    lax.fori_loop(1, half - 1, middle, 0)
-    arrive(half - 1, True)
-    compute(half - 1, 4, False, False)
-
-    for buf, kind in ((k_buf, RK), (p_buf, RP), (v_buf, LV)):
-        wait_for(kind, buf, half, 0)
-        for item in follow(half, 0, False, buf):
-            copy(*item).start()
+    lax.fori_loop(1, half - 2, middle, 0)
+    advance(half - 2, True)
+
+    compute(half - 1, 4, False, False, 0, KVH // 2)
+    arrive_last(k_buf, RK)
+    arrive_last(p_buf, RP)
+    compute(half - 1, 4, False, False, KVH // 2, KVH)
+    arrive_last(v_buf, LV)
     wait_for(SK0, k_buf, half, 1)
     wait_for(SP0, p_buf, half, 1)
     wait_for(SV0, v_buf, half, 1)
@@ -213,11 +239,12 @@
             pltpu.VMEM((slots, 4 * rows, keys.shape[1]), jnp.bfloat16),
             pltpu.VMEM((slots, 4 * rows, keys.shape[1]), jnp.bfloat16),
             pltpu.VMEM((slots, 4, 8, rows), jnp.int32),
-            pltpu.VMEM((4 * rows, rows), jnp.float32),
-            pltpu.VMEM((8, rows), jnp.int32),
-            pltpu.VMEM((width // (2 * HD), HD, 2 * rows), jnp.float32),
-            pltpu.VMEM((width // (2 * HD), 1, 2 * rows), jnp.float32),
-            pltpu.VMEM((width // (2 * HD), 1, 2 * rows), jnp.float32),
+            pltpu.VMEM((rows, 4 * rows), jnp.float32),
+            pltpu.VMEM((rows, 1), jnp.int32),
+            pltpu.VMEM((rows, 1), jnp.int32),
+            pltpu.VMEM((rows, width), jnp.float32),
+            pltpu.VMEM((rows, width), jnp.float32),
+            pltpu.VMEM((rows, width), jnp.float32),
             pltpu.SemaphoreType.DMA((12, slots)),
             pltpu.SemaphoreType.DMA((12, slots)),
         ],

time: 85 us -> 64.9 us (0.76)
  Pallas kernels: 81.7 us -> 61.6 us
    pallas_call x1, Pallas kernels: 81.7 us -> 61.6 us  [ring_attend(): pl.pallas_call(functools.partial(ring_attend_kernel, chips, depth), out_s...]
where the time goes in v4:
time: 64.9 us; the launch traced here: 64.7 us
  Pallas kernels  61.6 us (95%)
  local copies, waits for them, and re-layouts  3.1 us (5%)
    pallas_call x1, Pallas kernels, ring_attend(): pl.pallas_call(functools.partial(ring_attend_kernel, chips, depth), out_s...  61.6 us
    unnamed x1, local copies, waits for them, and re-layouts  3.1 us

profile of v4, /device:TPU:0, one launch (start us, length us, event | category | flops | bytes accessed | tf_op | source)
XLA Modules:
  0.0 64.7 jit_solution(2235706474929617004)
XLA Ops:
  0.0 61.6 %shard_map.55 = bf16[128,8192]{1,0:T(8,128)(2,1)} custom-call(bf16[128,8192]{1,0:T(8,128)(2,1)} %q_ref.1, bf16[128,1024]{1,0:T(8,128)(2,1)} %k_ref.1, bf16[128,1024]{1,0:T(8,128)(2,1)} %v_ref.1, s32[8]{0:T(128)} %blocks_ref.1, s32[1,2048]{1,0:T(1,128)} %bitcast.1), custom_call_target="tpu_custom_call" | custom-call | tf_op jit(solution)/shard_map/pallas_call | solution.py:233
  61.6 3.1 %copy.7 = bf16[128,8192]{1,0:T(8,128)(2,1)} copy(bf16[128,8192]{1,0:T(8,128)(2,1)} %shard_map.55) | data formatting | bytes 4194304
